TPU v7x, 512 devices: a whole 4x8x8 slice. The times are simulated.
512 devices in a mesh: prow: 32 (over y, z_lo, core), pcol: 16 (over z_hi, x).
Axes of the slice: x: 4, y: 8, z: 8 (z_hi: 4, z_lo: 2; z = z_hi * 2 + z_lo), core: 2. Of those that a mesh axis runs over, the one named last changes fastest.
Arguments:
- inverse_blocks: bfloat16 [24576, 24576], P('prow', 'pcol'), may hold values from -0.0390625 to 0.0390625
- lower_panel: bfloat16 [2, 24576, 384], P(None, 'prow', 'pcol'), may hold values from -0.75 to 0.75
- diag_inverse: float32 [2, 384, 384], P(None, None, 'pcol'), may hold values from -6 to 6
- structure: int32 [2, 48], replicated, may hold values from 0 to 63, all different within a row
Outputs:
- selected_column: float32 [2, 24576, 384], P(None, 'prow', 'pcol')
- diagonal_block: float32 [2, 384, 384], P(None, None, 'pcol')
Inputs may be any that keep to these rules, and one draw needn't show every extreme that they name: `structure`: each row names 48 different block numbers; every block number appears in some row.
All inputs are finite; a program needn't handle non-finite values.
Results may differ from a plain program's by a relative error of at most 0.0003.
Values may be sent and summed in bfloat16 or wider, within the bound.
A program may use at most 64 MiB of HBM per device.

v0:
```python
import jax
import jax.numpy as jnp
from jax import lax
from jax.sharding import PartitionSpec as P

W = 384


def spread(shard, axis, root):
    mine = lax.axis_index(axis) == root
    return lax.psum(jnp.where(mine, shard, jnp.zeros_like(shard)), axis)


def body(inverse_blocks, lower_panel, diag_inverse, structure):
    root_count = lax.axis_size("prow") // lax.axis_size("pcol")
    blocks_dev = lower_panel.shape[1] // W
    block_total = blocks_dev * lax.axis_size("prow")
    block_ids = jnp.arange(block_total, dtype=jnp.int32)
    matches = (structure[:, :, None] == block_ids[None, None, :]).astype(jnp.float32)
    present = jnp.minimum(jnp.sum(matches, axis=1), 1.0)
    own_blocks = lax.dynamic_slice_in_dim(
        present, lax.axis_index("prow") * blocks_dev, blocks_dev, 1
    )
    own_rows = jnp.repeat(own_blocks, W, axis=1)
    masked = (lower_panel.astype(jnp.float32) * own_rows[:, :, None]).astype(jnp.bfloat16)
    full_panel = lax.all_gather(masked, "pcol", axis=2, tiled=True)
    column_base = lax.axis_index("pcol") * root_count
    pieces = []
    for offset in range(root_count):
        pieces.append(spread(full_panel, "prow", column_base + offset))
    gathered = jnp.concatenate(pieces, axis=1)
    partial_value = jnp.einsum(
        "rc,scw->srw", inverse_blocks, gathered, preferred_element_type=jnp.float32
    )
    summed = lax.psum_scatter(partial_value, "pcol", scatter_dimension=2, tiled=True)
    selected_column = -(summed * own_rows[:, :, None])
    diag_term = jnp.einsum(
        "srw,srv->swv",
        full_panel.astype(jnp.float32),
        selected_column,
        precision=lax.Precision.HIGHEST,
    )
    diagonal_block = diag_inverse - lax.psum(diag_term, "prow")
    return (selected_column, diagonal_block)


def solution(mesh):
    in_specs = (P("prow", "pcol"), P(None, "prow", "pcol"), P(None, None, "pcol"), P())
    out_specs = (P(None, "prow", "pcol"), P(None, None, "pcol"))
    return jax.shard_map(body, mesh=mesh, in_specs=in_specs, out_specs=out_specs, check_vma=False)
```

profile of v0, /device:TPU:1, one launch (start us, length us, event | category | flops | bytes accessed | tf_op | source)
XLA Modules:
  0.0 623.4 jit_solution(4055498524274950222)
XLA Ops:
  7.2 0.0 copy-start
  7.2 0.0 all-gather.2.cloned.1.call-start
  7.2 0.9 convert_reduce_fusion
  8.2 0.1 constant_dynamic-slice_fusion
  8.2 0.1 broadcast_bitcast_fusion
  8.3 1.5 multiply_convert_fusion
  9.9 0.0 all-gather.2.cloned.1.call-update
  9.9 0.0 all-reduce.6.cloned.1.call-start
  9.9 66.0 %all-gather.2.cloned.1.call-done = bf16[2,768,384]{1,2,0:T(8,128)(2,1)} async-done(((bf16[2,768,24]{1,2,0:T(8,128)(2,1)}), bf16[2,768,384]{1,2,0:T(8,128)(2,1)}) %all-gather.2.cloned.1.call-update) | async-done | bytes 1179664 | tf_op jit(solution)/shard_map/all_gather | solution.py:26
  76.0 2.8 broadcast_select_fusion.1
  78.8 0.0 all-reduce.6.cloned.1.call-update
  78.8 0.0 reduce-scatter.2.cloned.1.call-start
  78.9 236.0 %all-reduce.6.cloned.1.call-done = (bf16[2,768,384]{1,2,0:T(8,128)(2,1)}, bf16[2,768,384]{1,2,0:T(8,128)(2,1)}) async-done(((bf16[2,768,384]{1,2,0:T(8,128)(2,1)}, bf16[2,768,384]{1,2,0:T(8,128)(2,1)}), (bf16[2,768,384]{1,2,0:T(8,128)(2,1)}, bf16[2,768,384]{1,2,0:T(8,128)(2,1)})) %all-reduce.6.cloned.1.call-update) | async-done | bytes 2359312 | tf_op jit(solution)/shard_map/psum | solution.py:11
  314.9 0.0 copy-done
  314.9 5.1 fusion.5
  319.9 0.0 copy-start.1
  319.9 0.0 reduce-scatter.2.cloned.1.call-update
  320.0 0.0 all-reduce.4.cloned.1.call-start
  320.0 95.0 %reduce-scatter.2.cloned.1.call-done = f32[2,768,24]{1,2,0:T(8,128)} async-done(((f32[2,768,384]{1,2,0:T(8,128)}), f32[2,768,24]{1,2,0:T(8,128)}) %reduce-scatter.2.cloned.1.call-update) | async-done | bytes 147472 | tf_op jit(solution)/shard_map/reduce_scatter | solution.py:35
  415.0 0.9 multiply_negate_fusion
  416.0 0.0 copy-start.2
  416.0 0.7 copy-done.2
  416.6 0.0 copy-done.1
  416.6 1.7 fusion.11
  418.3 0.0 all-reduce.4.cloned.1.call-update
  418.3 197.0 %all-reduce.4.cloned.1.call-done = f32[2,384,24]{1,2,0:T(8,128)} async-done(((f32[2,384,24]{1,2,0:T(8,128)}), f32[2,384,24]{1,2,0:T(8,128)}) %all-reduce.4.cloned.1.call-update) | async-done | bytes 73744 | tf_op jit(solution)/shard_map/psum | solution.py:43
  615.3 1.6 sub.3
  (2 shorter events, 0.0 us)
Async XLA Ops:
  7.2 307.7 %copy-start = (bf16[768,1536]{1,0:T(8,128)(2,1)S(1)}, bf16[768,1536]{1,0:T(8,128)(2,1)}, u32[]{:S(2)}) copy-start(bf16[768,1536]{1,0:T(8,128)(2,1)} %param.4) | copy-start | bytes 7077892
  7.2 68.8 %all-gather.2.cloned.1.call-start = ((), (), s32[]{:S(2)}) async-start(), calls=%async_computation.1 | async-start | bytes 1253376 | tf_op jit(solution)/shard_map/all_gather | solution.py:26
  9.9 305.0 %all-reduce.6.cloned.1.call-start = ((), (), s32[]{:S(2)}) async-start(), calls=%async_computation.4 | async-start | bytes 4718592 | tf_op jit(solution)/shard_map/psum | solution.py:11
  78.8 336.2 %reduce-scatter.2.cloned.1.call-start = ((), (), s32[]{:S(2)}) async-start(), calls=%async_computation.2 | async-start | bytes 2506752 | tf_op jit(solution)/shard_map/reduce_scatter | solution.py:35
  319.9 96.7 %copy-start.1 = (bf16[2,768,384]{1,2,0:T(8,128)(2,1)S(1)}, bf16[2,768,384]{1,2,0:T(8,128)(2,1)}, u32[]{:S(2)}) copy-start(bf16[2,768,384]{1,2,0:T(8,128)(2,1)} %all-gather.2.cloned.1.call-done) | copy-start | bytes 3538948
  320.0 295.3 %all-reduce.4.cloned.1.call-start = ((), (), s32[]{:S(2)}) async-start(), calls=%async_computation.3 | async-start | bytes 147456 | tf_op jit(solution)/shard_map/psum | solution.py:43
  416.0 0.7 copy-start.2
Sparse Core Ops, SparseCore 0:
  11.7 64.2 all-gather.1
  78.9 235.8 all-reduce.5
  320.1 94.8 reduce-scatter.1
  418.4 196.7 all-reduce.3
where the time goes:
time: 624 us; the launch traced here: 623 us
  waiting for transfers between devices  594 us (95%)
  between operations  13.8 us (2%)
  other arithmetic  7.78 us (1%)
  matrix products  6.72 us (1%)
    psum x1, waiting for transfers between devices, spread(): return lax.psum(jnp.where(mine, shard, jnp.zeros_like(shard)), axis)  236 us
    psum x1, waiting for transfers between devices, body(): diagonal_block = diag_inverse - lax.psum(diag_term, 'prow')  197 us
    reduce_scatter x1, waiting for transfers between devices, body(): lax.psum_scatter(partial_value, 'pcol', scatter_dimension=2, tiled=True)  95 us
    all_gather x1, waiting for transfers between devices, body(): full_panel = lax.all_gather(masked, 'pcol', axis=2, tiled=True)  66 us
  transfers between devices with their start and end apart: 4, of which 4 were waited for; matrix products, arithmetic and copies ran while one was open for 0% of the time, Pallas kernels for 0%

commit v1 on v0

v1 whole, which is shorter than its diff:
```python
import functools

import jax
import jax.numpy as jnp
from jax import lax
from jax.experimental import pallas as pl
from jax.experimental.pallas import tpu as pltpu
from jax.sharding import PartitionSpec as P

MESH = pl.DeviceIdType.MESH
F32, BF16, I16, I32 = jnp.float32, jnp.bfloat16, jnp.int16, jnp.int32
SNODES = 2
X = 4
NT = (((1,), (1,)), ((), ()))
TINY = 1e-33


def encode(value):
    top = jnp.maximum(jnp.max(jnp.abs(value), axis=0, keepdims=True), TINY)
    code = jnp.round(value * (32767.0 / top)).astype(I32).astype(I16)
    return code, top * (1.0 / 32767.0)


def decode(code, scale):
    return code.astype(I32).astype(F32) * scale


def kernel(
    rows_n, cols_n, a_hbm, l_ref, dinv_ref, struct_ref, sel_ref, diag_ref,
    a_ref, own, panel, prod, xs, xs_scale, xr, xr_scale, acc, zs, zs_scale, zr, zr_scale,
    ts, ts_scale, tr, tr_scale, sorted_panel, dpart, dsum_in, dtile, dfin,
    a_sem, l_sem, zl_sem, sib_send, sib_recv, ring_send, ring_recv, x_send, x_recv, z_send, z_recv,
    t_sem, rs_send, rs_recv, ag_send, ag_recv,
):
    wide = l_ref.shape[1]
    rows = l_ref.shape[2]
    vb = SNODES * wide
    nq = cols_n
    y_n = rows_n // 4
    zh_n = nq // X
    half = y_n // 2
    tiles_across = nq * wide // 128
    tiles = (vb // 8) * tiles_across

    prow, q = lax.axis_index("prow"), lax.axis_index("pcol")
    p, core = prow // 2, prow % 2
    y, zl = p // 2, p % 2
    zh, x = q // X, q % X
    depth = lax.rem(y - q // 2 + y_n, y_n)
    mine = 2 * depth + (zl + q) % 2

    def row_of(yy, zz, cc):
        return lax.rem(yy + y_n, y_n) * 4 + zz * 2 + cc

    partner = (row_of(p // 2 + q // 2, (p + q) % 2, core), p)
    source = (q * 2 + core, mine)
    is_self = jnp.logical_and(partner[0] == prow, partner[1] == q)
    up, down = (row_of(y + 1, zl, core), q), (row_of(y - 1, zl, core), q)
    across = (row_of(y, 1 - zl, core), q)
    sibling = (row_of(y, zl, 1 - core), q)
    xpeer = [(prow, zh * X + lax.rem(x + o, X)) for o in range(1, X)]
    zpeer = [(prow, lax.rem(zh + o, zh_n) * X + x) for o in range(1, zh_n)]

    load_a = pltpu.make_async_copy(a_hbm, a_ref, a_sem)
    load_a.start()

    barrier = pltpu.get_barrier_semaphore()
    fixed = [up, down, across, sibling] + xpeer + zpeer
    for device in fixed:
        pl.semaphore_signal(barrier, inc=1, device_id=device, device_id_type=MESH)

    @pl.when(jnp.logical_not(is_self))
    def _():
        pl.semaphore_signal(barrier, inc=1, device_id=partner, device_id_type=MESH)
        pl.semaphore_signal(barrier, inc=1, device_id=source, device_id_type=MESH)

    lane = lax.broadcasted_iota(I32, (1, rows), 1)
    table = struct_ref[...]
    marks = []
    for s in range(SNODES):
        hits = [
            jnp.max((table[s : s + 1, :] == prow * 2 + b).astype(F32), axis=1, keepdims=True) for b in range(2)
        ]
        marks.append(jnp.where(lane < rows // 2, hits[0], hits[1]))
    mask = jnp.concatenate([jnp.broadcast_to(m, (wide, rows)) for m in marks], axis=0)
    raw = jnp.concatenate([l_ref[s].astype(F32) for s in range(SNODES)], axis=0)
    own[...] = (raw * mask).astype(BF16)

    @pl.when(is_self)
    def _():
        pl.semaphore_wait(barrier, len(fixed))

    @pl.when(jnp.logical_not(is_self))
    def _():
        pl.semaphore_wait(barrier, len(fixed) + 2)

    started = []

    def send(src, dst, send_sem, recv_sem, device):
        copy = pltpu.make_async_remote_copy(
            src_ref=src, dst_ref=dst, send_sem=send_sem, recv_sem=recv_sem, device_id=device, device_id_type=MESH
        )
        copy.start()
        started.append(copy)
        return copy

    def block(index, first=0, count=2):
        start = pl.multiple_of((lax.rem(index + y_n, y_n) * 2 + first) * vb, 16)
        return panel.at[core, pl.ds(start, count * vb), :]

    def other(index, first=0, count=2):
        start = pl.multiple_of((lax.rem(index + y_n, y_n) * 2 + first) * vb, 16)
        return panel.at[1 - core, pl.ds(start, count * vb), :]

    def slot(index):
        return panel.at[core, pl.ds(pl.multiple_of(index * vb, 16), vb), :]

    def hand_over(src, dst, sems, recv_dst):
        @pl.when(is_self)
        def _():
            copy = pltpu.make_async_copy(src, dst, sems.at[2])
            copy.start()
            copy.wait()

        @pl.when(jnp.logical_not(is_self))
        def _():
            copy = pltpu.make_async_remote_copy(
                src_ref=src, dst_ref=dst, send_sem=sems.at[0], recv_sem=sems.at[1],
                device_id=partner, device_id_type=MESH,
            )
            copy.start()
            copy.wait_send()
            pltpu.make_async_remote_copy(
                src_ref=src, dst_ref=recv_dst, send_sem=sems.at[0], recv_sem=sems.at[1],
                device_id=partner, device_id_type=MESH,
            ).wait_recv()

    hand_over(own, slot(q), l_sem, slot(mine))

    pair = send(slot(mine), slot(mine), zl_sem.at[0], zl_sem.at[1], across)
    pair.wait_recv()

    sib = []

    def to_sibling(index, first=0, count=2):
        k = len(sib)
        send(block(index, first, count), block(index, first, count), sib_send.at[k], sib_recv.at[k], sibling)
        sib.append((index, first, count))

    def wait_sibling(k):
        piece = other(*sib[k])
        pltpu.make_async_remote_copy(
            src_ref=piece, dst_ref=piece, send_sem=sib_send.at[k], recv_sem=sib_recv.at[k],
            device_id=sibling, device_id_type=MESH,
        ).wait_recv()

    def ring(t):
        part_up, part_down = ((0, 2), (0, 2)) if t < half else ((0, 1), (1, 1))
        src_up, src_down = block(depth - (t - 1), *part_up), block(depth + (t - 1), *part_down)
        send(src_up, src_up, ring_send.at[0, t - 1], ring_recv.at[0, t - 1], up)
        send(src_down, src_down, ring_send.at[1, t - 1], ring_recv.at[1, t - 1], down)

    def ring_wait(t):
        part_up, part_down = ((0, 2), (0, 2)) if t < half else ((0, 1), (1, 1))
        dst_up, dst_down = block(depth - t, *part_up), block(depth + t, *part_down)
        for way, dst, device in ((0, dst_up, up), (1, dst_down, down)):
            pltpu.make_async_remote_copy(
                src_ref=dst, dst_ref=dst, send_sem=ring_send.at[way, t - 1], recv_sem=ring_recv.at[way, t - 1],
                device_id=device, device_id_type=MESH,
            ).wait_recv()

    for t in range(1, half + 1):
        ring(t)
        if t == 1:
            to_sibling(depth)
        else:
            to_sibling(depth - (t - 1))
            to_sibling(depth + (t - 1))
        ring_wait(t)
    to_sibling(depth + half)
    for k in range(len(sib)):
        wait_sibling(k)
    load_a.wait()

    for g in range(zh_n):
        group = pl.ds(g * X * vb, X * vb)
        prod[g] = lax.dot_general(
            panel[0, group, :], a_ref[:, :rows], NT, preferred_element_type=F32
        ) + lax.dot_general(panel[1, group, :], a_ref[:, rows:], NT, preferred_element_type=F32)
        for o in range(1, X):
            to = lax.rem(x + o, X)
            code, scale = encode(prod[g, pl.ds(pl.multiple_of(to * vb, 8), vb), :])
            xs[g, o - 1] = code
            xs_scale[g, o - 1] = scale
            send(xs.at[g, o - 1], xr.at[g, o - 1], x_send.at[0, g, o - 1], x_recv.at[0, g, o - 1], xpeer[o - 1])
            send(
                xs_scale.at[g, o - 1], xr_scale.at[g, o - 1],
                x_send.at[1, g, o - 1], x_recv.at[1, g, o - 1], xpeer[o - 1],
            )

    def wait_for(dst, send_sem, recv_sem, device):
        pltpu.make_async_remote_copy(
            src_ref=dst, dst_ref=dst, send_sem=send_sem, recv_sem=recv_sem, device_id=device, device_id_type=MESH
        ).wait_recv()

    for s in range(SNODES):
        for k in range(0, nq, 2):
            pieces = [panel[core, (k + i) * vb : (k + i + 1) * vb, :].astype(F32) for i in range(2)]
            both = jnp.concatenate([piece[s * wide : (s + 1) * wide] for piece in pieces], axis=0)
            sorted_panel[s, k * wide : (k + 2) * wide, :] = both.astype(BF16)

    for g in range(zh_n):
        total = prod[g, pl.ds(pl.multiple_of(x * vb, 8), vb), :]
        for o in range(X - 1):
            wait_for(xr.at[g, o], x_send.at[0, g, o], x_recv.at[0, g, o], xpeer[o])
            wait_for(xr_scale.at[g, o], x_send.at[1, g, o], x_recv.at[1, g, o], xpeer[o])
            total = total + decode(xr[g, o], xr_scale[g, o])
        acc[g] = total

    for o in range(1, zh_n):
        code, scale = encode(acc[lax.rem(zh + o, zh_n)])
        zs[o - 1] = code
        zs_scale[o - 1] = scale
        send(zs.at[o - 1], zr.at[o - 1], z_send.at[0, o - 1], z_recv.at[0, o - 1], zpeer[o - 1])
        send(zs_scale.at[o - 1], zr_scale.at[o - 1], z_send.at[1, o - 1], z_recv.at[1, o - 1], zpeer[o - 1])
    total = acc[zh]
    for o in range(zh_n - 1):
        wait_for(zr.at[o], z_send.at[0, o], z_recv.at[0, o], zpeer[o])
        wait_for(zr_scale.at[o], z_send.at[1, o], z_recv.at[1, o], zpeer[o])
        total = total + decode(zr[o], zr_scale[o])
    sel = -(total * mask)
    for s in range(SNODES):
        sel_ref[s] = sel[s * wide : (s + 1) * wide]

    code, scale = encode(sel)
    ts[...] = code
    ts_scale[...] = scale
    hand_over(ts, tr, t_sem.at[0], tr)
    hand_over(ts_scale, tr_scale, t_sem.at[1], tr_scale)
    moved = decode(tr[...], tr_scale[...])
    high = moved.astype(BF16)
    low = (moved - high.astype(F32)).astype(BF16)
    for s in range(SNODES):
        part = slice(s * wide, (s + 1) * wide)
        term = lax.dot_general(high[part], sorted_panel[s], NT, preferred_element_type=F32) + lax.dot_general(
            low[part], sorted_panel[s], NT, preferred_element_type=F32
        )
        for i in range(wide // 8):
            for k in range(tiles_across):
                dpart[(s * (wide // 8) + i) * tiles_across + k] = term[i * 8 : i * 8 + 8, k * 128 : k * 128 + 128]

    number = q + nq * core

    def scatter(j, carry):
        c, cc = lax.rem(j, nq), j // nq
        there = (row_of(c // 2 + mine // 2, (c + mine) % 2, cc), c)
        same = jnp.logical_and(there[0] == prow, there[1] == q)

        @pl.when(same)
        def _():
            pltpu.make_async_copy(dpart.at[j], dsum_in.at[number], rs_recv.at[number]).start()

        @pl.when(jnp.logical_not(same))
        def _():
            pltpu.make_async_remote_copy(
                src_ref=dpart.at[j], dst_ref=dsum_in.at[number], send_sem=rs_send.at[j],
                recv_sem=rs_recv.at[number], device_id=there, device_id_type=MESH,
            ).start()

        return carry

    lax.fori_loop(0, tiles, scatter, 0)

    @pl.when(number < tiles)
    def _():
        def take(k, carry):
            pltpu.make_async_copy(dsum_in.at[k], dsum_in.at[k], rs_recv.at[k]).wait()
            return carry

        lax.fori_loop(0, 2 * nq, take, 0)
        dtile[...] = jnp.sum(dsum_in[...], axis=0)

        def give(i, carry):
            same = jnp.logical_and(i == prow, mine == q)

            @pl.when(same)
            def _():
                pltpu.make_async_copy(dtile, dfin.at[number], ag_recv.at[number]).start()

            @pl.when(jnp.logical_not(same))
            def _():
                pltpu.make_async_remote_copy(
                    src_ref=dtile, dst_ref=dfin.at[number], send_sem=ag_send.at[i],
                    recv_sem=ag_recv.at[number], device_id=(i, mine), device_id_type=MESH,
                ).start()

            return carry

        lax.fori_loop(0, rows_n, give, 0)

    def collect(j, carry):
        pltpu.make_async_copy(dfin.at[j], dfin.at[j], ag_recv.at[j]).wait()
        return carry

    lax.fori_loop(0, tiles, collect, 0)
    for s in range(SNODES):
        for i in range(wide // 8):
            for k in range(tiles_across):
                here = (s, slice(i * 8, i * 8 + 8), slice(k * 128, k * 128 + 128))
                diag_ref[here] = dinv_ref[here] - dfin[(s * (wide // 8) + i) * tiles_across + k]

    for copy in started:
        copy.wait_send()

    def scatter_done(j, carry):
        c, cc = lax.rem(j, nq), j // nq
        there = (row_of(c // 2 + mine // 2, (c + mine) % 2, cc), c)

        @pl.when(jnp.logical_not(jnp.logical_and(there[0] == prow, there[1] == q)))
        def _():
            pltpu.make_async_copy(dpart.at[j], dpart.at[j], rs_send.at[j]).wait()

        return carry

    lax.fori_loop(0, tiles, scatter_done, 0)

    @pl.when(number < tiles)
    def _():
        def give_done(i, carry):
            @pl.when(jnp.logical_not(jnp.logical_and(i == prow, mine == q)))
            def _():
                pltpu.make_async_copy(dtile, dtile, ag_send.at[i]).wait()

            return carry

        lax.fori_loop(0, rows_n, give_done, 0)


def body(rows_n, cols_n, inverse_blocks, lower_panel, diag_inverse, structure):
    panel_t = jnp.swapaxes(lower_panel, 1, 2)
    dinv_t = jnp.swapaxes(diag_inverse, 1, 2)
    snodes, wide, rows = panel_t.shape
    vb = snodes * wide
    order = dinv_t.shape[2]
    zh_n = cols_n // X
    half = rows_n // 8
    tiles = (vb // 8) * (order // 128)
    vmem = pl.BlockSpec(memory_space=pltpu.VMEM)
    dma = pltpu.SemaphoreType.DMA
    sib_n = 1 + 2 * (half - 1) + 1
    sel_t, diag_t = pl.pallas_call(
        functools.partial(kernel, rows_n, cols_n),
        out_shape=(
            jax.ShapeDtypeStruct((snodes, wide, rows), F32),
            jax.ShapeDtypeStruct((snodes, wide, order), F32),
        ),
        in_specs=[pl.BlockSpec(memory_space=pl.ANY), vmem, vmem, vmem],
        out_specs=(vmem, vmem),
        scratch_shapes=[
            pltpu.VMEM(inverse_blocks.shape, BF16),
            pltpu.VMEM((vb, rows), BF16),
            pltpu.VMEM((2, cols_n * vb, rows), BF16),
            pltpu.VMEM((zh_n, X * vb, rows), F32),
            pltpu.VMEM((zh_n, X - 1, vb, rows), I16),
            pltpu.VMEM((zh_n, X - 1, 1, rows), F32),
            pltpu.VMEM((zh_n, X - 1, vb, rows), I16),
            pltpu.VMEM((zh_n, X - 1, 1, rows), F32),
            pltpu.VMEM((zh_n, vb, rows), F32),
            pltpu.VMEM((zh_n - 1, vb, rows), I16),
            pltpu.VMEM((zh_n - 1, 1, rows), F32),
            pltpu.VMEM((zh_n - 1, vb, rows), I16),
            pltpu.VMEM((zh_n - 1, 1, rows), F32),
            pltpu.VMEM((vb, rows), I16),
            pltpu.VMEM((1, rows), F32),
            pltpu.VMEM((vb, rows), I16),
            pltpu.VMEM((1, rows), F32),
            pltpu.VMEM((snodes, order, rows), BF16),
            pltpu.VMEM((tiles, 8, 128), F32),
            pltpu.VMEM((2 * cols_n, 8, 128), F32),
            pltpu.VMEM((8, 128), F32),
            pltpu.VMEM((tiles, 8, 128), F32),
            dma,
            dma((3,)),
            dma((2,)),
            dma((sib_n,)),
            dma((sib_n,)),
            dma((2, half)),
            dma((2, half)),
            dma((2, zh_n, X - 1)),
            dma((2, zh_n, X - 1)),
            dma((2, zh_n - 1)),
            dma((2, zh_n - 1)),
            dma((2, 3)),
            dma((tiles,)),
            dma((2 * cols_n,)),
            dma((rows_n,)),
            dma((tiles,)),
        ],
        compiler_params=pltpu.CompilerParams(
            collective_id=0, has_side_effects=True, vmem_limit_bytes=40 * 1024 * 1024
        ),
    )(inverse_blocks, panel_t, dinv_t, structure)
    return jnp.swapaxes(sel_t, 1, 2), jnp.swapaxes(diag_t, 1, 2)


def solution(mesh):
    in_specs = (P("prow", "pcol"), P(None, "prow", "pcol"), P(None, None, "pcol"), P())
    out_specs = (P(None, "prow", "pcol"), P(None, None, "pcol"))
    step = functools.partial(body, mesh.shape["prow"], mesh.shape["pcol"])
    return jax.shard_map(step, mesh=mesh, in_specs=in_specs, out_specs=out_specs, check_vma=False)
```

time: 624 us -> 111 us (0.18)
  waiting for transfers between devices: 594 us -> 0 us
  Pallas kernels: 0 us -> 105 us
  between operations: 13.8 us -> 0.65 us
  other arithmetic: 7.78 us -> 0 us
  matrix products: 6.72 us -> 0 us
    psum x2 -> x0, waiting for transfers between devices: 433 us -> none  [the longest x1 236 us: spread(): return lax.psum(jnp.where(mine, shard, jnp.zeros_like(shard)), axis)]
    pallas_call x0 -> x1, Pallas kernels: none -> 105 us  [body(): pl.pallas_call(functools.partial(kernel, rows_n, cols_n), out_shape=(jax....]
    reduce_scatter x1 -> x0, waiting for transfers between devices: 95 us -> none  [body(): lax.psum_scatter(partial_value, 'pcol', scatter_dimension=2, tiled=True)]
    all_gather x1 -> x0, waiting for transfers between devices: 66 us -> none  [body(): full_panel = lax.all_gather(masked, 'pcol', axis=2, tiled=True)]
    dot_general x2 -> x0, matrix products: 6.72 us -> none  [the longest x1 5.06 us: body(): jnp.einsum('rc,scw->srw', inverse_blocks, gathered, preferred_element_typ...]
  transfers between devices with their start and end apart: 4 -> 0, of which waited for: 4 -> 0; matrix products, arithmetic and copies ran while one was open for 0% -> 0% of each run, Pallas kernels for 0% -> 0%
where the time goes in v1:
time: 111 us
  Pallas kernels  105 us (95%)
  local copies, waits for them, and re-layouts  5.4 us (5%)
    pallas_call x1, Pallas kernels, body(): pl.pallas_call(functools.partial(kernel, rows_n, cols_n), out_shape=(jax....  105 us
    unnamed x10, local copies, waits for them, and re-layouts  5.4 us

profile of v1, /device:TPU:1, one launch (start us, length us, event | category | flops | bytes accessed | tf_op | source)
XLA Modules:
  0.0 111.1 jit_solution(16827913140985967818)
XLA Ops:
  0.6 0.0 copy-start
  0.6 1.7 %copy-done = bf16[768,1536]{1,0:T(8,128)(2,1)S(1)} copy-done((bf16[768,1536]{1,0:T(8,128)(2,1)S(1)}, bf16[768,1536]{1,0:T(8,128)(2,1)}, u32[]{:S(2)}) %copy-start) | copy-done | bytes 2359320
  2.3 0.0 copy-start.1
  2.3 0.9 copy-done.1
  3.2 0.0 copy-start.2
  3.2 0.9 copy-done.2
  4.1 0.0 copy-start.3
  4.1 0.7 copy-done.3
  4.7 105.1 %shard_map.59 = (f32[2,24,768]{2,1,0:T(8,128)S(1)}, f32[2,24,384]{2,1,0:T(8,128)S(1)}) custom-call(bf16[768,1536]{1,0:T(8,128)(2,1)S(1)} %copy-done, bf16[2,24,768]{2,1,0:T(8,128)(2,1)S(1)} %bitcast.5, f32[2,24,384]{2,1,0:T(8,128)S(1)} %bitcast.6, s32[2,48]{1,0:T(2,128)S(1)} %copy-done.3), custom_call_target="tpu_custom_call" | custom-call | tf_op jit(solution)/shard_map/pallas_call | solution.py:351
  109.8 0.7 copy.8
  110.5 0.6 copy.9
Async XLA Ops:
  0.6 1.7 %copy-start = (bf16[768,1536]{1,0:T(8,128)(2,1)S(1)}, bf16[768,1536]{1,0:T(8,128)(2,1)}, u32[]{:S(2)}) copy-start(bf16[768,1536]{1,0:T(8,128)(2,1)} %a_hbm.1) | copy-start | bytes 7077892
  2.3 0.9 copy-start.1
  3.2 0.9 copy-start.2
  4.1 0.7 copy-start.3

commit v2 on v1

v2 whole, which is shorter than its diff:
```python
import functools

import jax
import jax.numpy as jnp
from jax import lax
from jax.experimental import pallas as pl
from jax.experimental.pallas import tpu as pltpu
from jax.sharding import PartitionSpec as P

MESH = pl.DeviceIdType.MESH
F32, BF16, I16, I32 = jnp.float32, jnp.bfloat16, jnp.int16, jnp.int32
SNODES = 2
X = 4
NT = (((1,), (1,)), ((), ()))
TINY = 1e-33


def encode(value):
    top = jnp.maximum(jnp.max(jnp.abs(value), axis=0, keepdims=True), TINY)
    code = jnp.round(value * (32767.0 / top)).astype(I32).astype(I16)
    return code, top * (1.0 / 32767.0)


def decode(code, scale):
    return code.astype(I32).astype(F32) * scale


def kernel(
    rows_n, cols_n, a_hbm, l_ref, struct_ref, sel_ref, diag_ref,
    a_ref, panel, local, prod, xs, xs_scale, xr, xr_scale, acc, zs, zs_scale, zr, zr_scale,
    sorted_panel, dpart, dsum_in, dtile, dfin,
    load_sem, h_send, h_recv, y_send, y_recv, zl_send, zl_recv, sib_send, sib_recv, lz_send, lz_recv, lx_send, lx_recv,
    x_send, x_recv, z_send, z_recv, rs_send, rs_recv, ag_send, ag_recv,
):
    wide = l_ref.shape[1]
    rows = l_ref.shape[2]
    vb = SNODES * wide
    nq = cols_n
    y_n = rows_n // 4
    zh_n = nq // X
    tiles_across = nq * wide // 128
    tiles = (vb // 8) * tiles_across
    offsets = [0, -1, 1, -2, 2, -3, 3, 4]
    number_of = {offset: n for n, offset in enumerate(offsets)}

    prow, q = lax.axis_index("prow"), lax.axis_index("pcol")
    p, core = prow // 2, prow % 2
    y, zl = p // 2, p % 2
    zh, x = q // X, q % X
    depth = lax.rem(y - q // 2 + y_n, y_n)
    parity = (zl + q) % 2
    mine = 2 * depth + parity

    def row_of(yy, zz, cc):
        return lax.rem(yy + y_n, y_n) * 4 + zz * 2 + cc

    partner = (row_of(p // 2 + q // 2, (p + q) % 2, core), p)
    source = (q * 2 + core, mine)
    is_self = jnp.logical_and(partner[0] == prow, partner[1] == q)
    away = {o: (row_of(y + o, zl, core), q) for o in (1, -1, 2, -2)}
    across = (row_of(y, 1 - zl, core), q)
    sibling = (row_of(y, zl, 1 - core), q)
    xpeer = [(prow, zh * X + lax.rem(x + o, X)) for o in range(1, X)]
    zpeer = [(prow, lax.rem(zh + o, zh_n) * X + x) for o in range(1, zh_n)]

    barrier = pltpu.get_barrier_semaphore()
    fixed = [*away.values(), across, sibling] + xpeer + zpeer
    for device in fixed:
        pl.semaphore_signal(barrier, inc=1, device_id=device, device_id_type=MESH)

    @pl.when(jnp.logical_not(is_self))
    def _():
        pl.semaphore_signal(barrier, inc=1, device_id=partner, device_id_type=MESH)
        pl.semaphore_signal(barrier, inc=1, device_id=source, device_id_type=MESH)

    load_a = pltpu.make_async_copy(a_hbm, a_ref, load_sem)
    load_a.start()

    lane = lax.broadcasted_iota(I32, (1, rows), 1)
    table = struct_ref[...]
    marks = []
    for s in range(SNODES):
        hits = [
            jnp.max((table[s : s + 1, :] == prow * 2 + b).astype(F32), axis=1, keepdims=True) for b in range(2)
        ]
        marks.append(jnp.where(lane < rows // 2, hits[0], hits[1]))
    mask = jnp.concatenate([jnp.broadcast_to(m, (wide, rows)) for m in marks], axis=0)
    raw = jnp.concatenate([l_ref[s].astype(F32) for s in range(SNODES)], axis=0)
    own = local.at[pl.ds(pl.multiple_of(q * vb, 16), vb), :]
    own[...] = (raw * mask).astype(BF16)

    @pl.when(is_self)
    def _():
        pl.semaphore_wait(barrier, len(fixed))

    @pl.when(jnp.logical_not(is_self))
    def _():
        pl.semaphore_wait(barrier, len(fixed) + 2)

    started = []

    def send(src, dst, send_sem, recv_sem, device):
        copy = pltpu.make_async_remote_copy(
            src_ref=src, dst_ref=dst, send_sem=send_sem, recv_sem=recv_sem, device_id=device, device_id_type=MESH
        )
        copy.start()
        started.append(copy)

    def wait_for(dst, sem):
        pltpu.make_async_copy(dst, dst, sem).wait()

    def block(which, offset, side=0):
        index = lax.rem(depth + offset + y_n, y_n) * 2 + (parity if side == 0 else 1 - parity)
        return panel.at[which, pl.ds(pl.multiple_of(index * vb, 16), vb), :]

    def slot(index):
        return panel.at[core, pl.ds(pl.multiple_of(index * vb, 16), vb), :]

    def piece(index):
        return local.at[pl.ds(pl.multiple_of(index * vb, 16), vb), :]

    @pl.when(is_self)
    def _():
        pltpu.make_async_copy(own, slot(q), h_recv).start()

    @pl.when(jnp.logical_not(is_self))
    def _():
        pltpu.make_async_remote_copy(
            src_ref=own, dst_ref=slot(q), send_sem=h_send, recv_sem=h_recv, device_id=partner, device_id_type=MESH
        ).start()

    def start_local():
        for o in range(1, zh_n):
            send(own, own, lz_send.at[o - 1], lz_recv.at[o - 1], zpeer[o - 1])
        for o in range(1, X):
            send(own, own, lx_send.at[0, o - 1], lx_recv.at[0, o - 1], xpeer[o - 1])

    def pass_local(o):
        there = piece(lax.rem(zh - o + zh_n, zh_n) * X + x)
        wait_for(there, lz_recv.at[o - 1])
        for i in range(1, X):
            send(there, there, lx_send.at[o, i - 1], lx_recv.at[o, i - 1], xpeer[i - 1])

    start_local()
    wait_for(slot(mine), h_recv)

    def along_y(offset, arrives, device):
        src = block(core, offset)
        send(src, src, y_send.at[number_of[arrives]], y_recv.at[number_of[arrives]], device)

    def to_sibling(offset, side):
        n = number_of[offset]
        src = block(core, offset, side)
        send(src, src, sib_send.at[side, n], sib_recv.at[side, n], sibling)

    def spread(offset):
        n = number_of[offset]
        src = block(core, offset)
        send(src, src, zl_send.at[n], zl_recv.at[n], across)
        to_sibling(offset, 0)

    def take_y(offset):
        wait_for(block(core, offset), y_recv.at[number_of[offset]])

    def take_pair(offset):
        wait_for(block(core, offset, 1), zl_recv.at[number_of[offset]])
        to_sibling(offset, 1)

    along_y(0, -2, away[2])
    along_y(0, 2, away[-2])
    along_y(0, -1, away[1])
    along_y(0, 1, away[-1])
    spread(0)

    def multiply(offset):
        n = number_of[offset]
        for side in range(2):
            wait_for(block(1 - core, offset, side), sib_recv.at[side, n])
        b = lax.rem(depth + offset + y_n, y_n)
        group = pl.ds(pl.multiple_of(b * 2 * vb, 16), 2 * vb)
        prod[n] = lax.dot_general(
            panel[0, group, :], a_ref[:, :rows], NT, preferred_element_type=F32
        ) + lax.dot_general(panel[1, group, :], a_ref[:, rows:], NT, preferred_element_type=F32)
        for i in range(2):
            to = 2 * (b % 2) + i
            o = lax.rem(to - x + X, X)

            @pl.when(o == 0)
            def _():
                acc[b // 2] = prod[n, i * vb : (i + 1) * vb, :]

            @pl.when(o > 0)
            def _():
                code, scale = encode(prod[n, i * vb : (i + 1) * vb, :])
                xs[n, i] = code
                xs_scale[n, i] = scale
                for k, (src, dst) in enumerate(((xs, xr), (xs_scale, xr_scale))):
                    pltpu.make_async_remote_copy(
                        src_ref=src.at[n, i], dst_ref=dst.at[b // 2, o - 1], send_sem=x_send.at[k, n, i],
                        recv_sem=x_recv.at[k, b // 2, o - 1], device_id=(prow, zh * X + to), device_id_type=MESH,
                    ).start()

    high_x = x // 2
    odd = (depth + high_x) % 2
    sign = 1 - 2 * high_x

    def reduce_x(r):
        even_way, odd_way = ((0, -1), (-2, 1), (2, -3), (4, 3))[r - 1]
        b = lax.rem(depth + sign * ((1 - odd) * even_way + odd * odd_way) + y_n, y_n)
        g = b // 2
        total = acc[g]
        for o in range(X - 1):
            wait_for(xr.at[g, o], x_recv.at[0, g, o])
            wait_for(xr_scale.at[g, o], x_recv.at[1, g, o])
            total = total + decode(xr[g, o], xr_scale[g, o])
        o = lax.rem(g - zh + zh_n, zh_n)
        acc[g] = total

        @pl.when(o > 0)
        def _():
            code, scale = encode(acc[g])
            zs[o - 1] = code
            zs_scale[o - 1] = scale
            for k, (src, dst) in enumerate(((zs, zr), (zs_scale, zr_scale))):
                pltpu.make_async_remote_copy(
                    src_ref=src.at[o - 1], dst_ref=dst.at[o - 1], send_sem=z_send.at[k, o - 1],
                    recv_sem=z_recv.at[k, o - 1], device_id=(prow, g * X + x), device_id_type=MESH,
                ).start()

    take_pair(0)
    for offset in (-1, 1):
        take_y(offset)
        spread(offset)
    for offset in (-2, 2):
        take_y(offset)
        along_y(offset, 3 if offset > 0 else -3, away[-offset // 2])
    far = 1 - 2 * core
    index = lax.rem(depth - 2 * far + y_n, y_n) * 2 + parity
    across_ring = panel.at[core, pl.ds(pl.multiple_of(index * vb, 16), vb), :]
    send(across_ring, across_ring, y_send.at[7], y_recv.at[7], (row_of(y + 2 * far, zl, core), q))
    for offset in (-2, 2):
        spread(offset)
    for o in range(1, zh_n):
        pass_local(o)
    load_a.wait()
    multiply(0)
    for offset in (-1, 1):
        take_pair(offset)
        multiply(offset)
    for offset in (-3, 3, 4):
        take_y(offset)
        spread(offset)
    for r in (2, 3):
        for offset in (-r, r):
            take_pair(offset)
            multiply(offset)
    reduce_x(1)
    take_pair(4)
    multiply(4)
    reduce_x(2)
    reduce_x(3)

    for o in range(zh_n):
        for i in range(1, X):
            wait_for(
                piece(lax.rem(zh - o + zh_n, zh_n) * X + lax.rem(x - i + X, X)), lx_recv.at[o, i - 1]
            )
    for s in range(SNODES):
        for k in range(0, nq, 2):
            pieces = [local[(k + i) * vb : (k + i + 1) * vb, :].astype(F32) for i in range(2)]
            both = jnp.concatenate([part[s * wide : (s + 1) * wide] for part in pieces], axis=0)
            sorted_panel[s, k * wide : (k + 2) * wide, :] = both.astype(BF16)

    reduce_x(4)
    total = acc[zh]
    for o in range(zh_n - 1):
        wait_for(zr.at[o], z_recv.at[0, o])
        wait_for(zr_scale.at[o], z_recv.at[1, o])
        total = total + decode(zr[o], zr_scale[o])
    sel = -(total * mask)
    for s in range(SNODES):
        sel_ref[s] = sel[s * wide : (s + 1) * wide]

    high = sel.astype(BF16)
    low = (sel - high.astype(F32)).astype(BF16)
    for s in range(SNODES):
        part = slice(s * wide, (s + 1) * wide)
        term = lax.dot_general(high[part], sorted_panel[s], NT, preferred_element_type=F32) + lax.dot_general(
            low[part], sorted_panel[s], NT, preferred_element_type=F32
        )
        for i in range(wide // 8):
            for k in range(tiles_across):
                dpart[(s * (wide // 8) + i) * tiles_across + k] = term[i * 8 : i * 8 + 8, k * 128 : k * 128 + 128]

    chips = rows_n // 2
    number = p + chips * core

    def handler(j):
        return lax.rem(j, chips) * 2 + j // chips

    def scatter(j, carry):
        there = handler(j)

        @pl.when(there == prow)
        def _():
            pltpu.make_async_copy(dpart.at[j], dsum_in.at[prow], rs_recv.at[prow]).start()

        @pl.when(there != prow)
        def _():
            pltpu.make_async_remote_copy(
                src_ref=dpart.at[j], dst_ref=dsum_in.at[prow], send_sem=rs_send.at[j],
                recv_sem=rs_recv.at[prow], device_id=(there, q), device_id_type=MESH,
            ).start()

        return carry

    lax.fori_loop(0, tiles, scatter, 0)

    @pl.when(number < tiles)
    def _():
        def take(k, carry):
            wait_for(dsum_in.at[k], rs_recv.at[k])
            return carry

        lax.fori_loop(0, rows_n, take, 0)
        dtile[...] = jnp.sum(dsum_in[...], axis=0)

        def give(i, carry):
            @pl.when(i == prow)
            def _():
                pltpu.make_async_copy(dtile, dfin.at[number], ag_recv.at[number]).start()

            @pl.when(i != prow)
            def _():
                pltpu.make_async_remote_copy(
                    src_ref=dtile, dst_ref=dfin.at[number], send_sem=ag_send.at[i],
                    recv_sem=ag_recv.at[number], device_id=(i, q), device_id_type=MESH,
                ).start()

            return carry

        lax.fori_loop(0, rows_n, give, 0)

    def collect(j, carry):
        wait_for(dfin.at[j], ag_recv.at[j])
        return carry

    lax.fori_loop(0, tiles, collect, 0)
    for s in range(SNODES):
        for i in range(wide // 8):
            for k in range(tiles_across):
                here = (s, slice(i * 8, i * 8 + 8), slice(k * 128, k * 128 + 128))
                diag_ref[here] = dfin[(s * (wide // 8) + i) * tiles_across + k]

    for copy in started:
        copy.wait_send()

    @pl.when(jnp.logical_not(is_self))
    def _():
        wait_for(own, h_send)

    for offset in offsets:
        n = number_of[offset]
        b = lax.rem(depth + offset + y_n, y_n)
        for i in range(2):
            @pl.when(2 * (b % 2) + i != x)
            def _():
                wait_for(xs.at[n, i], x_send.at[0, n, i])
                wait_for(xs_scale.at[n, i], x_send.at[1, n, i])

    for o in range(zh_n - 1):
        wait_for(zs.at[o], z_send.at[0, o])
        wait_for(zs_scale.at[o], z_send.at[1, o])

    def scatter_done(j, carry):
        @pl.when(handler(j) != prow)
        def _():
            wait_for(dpart.at[j], rs_send.at[j])

        return carry

    lax.fori_loop(0, tiles, scatter_done, 0)

    @pl.when(number < tiles)
    def _():
        def give_done(i, carry):
            @pl.when(i != prow)
            def _():
                wait_for(dtile, ag_send.at[i])

            return carry

        lax.fori_loop(0, rows_n, give_done, 0)


def body(rows_n, cols_n, inverse_blocks, lower_panel, diag_inverse, structure):
    panel_t = jnp.swapaxes(lower_panel, 1, 2)
    snodes, wide, rows = panel_t.shape
    vb = snodes * wide
    order = diag_inverse.shape[1]
    zh_n = cols_n // X
    y_n = rows_n // 4
    tiles = (vb // 8) * (order // 128)
    vmem = pl.BlockSpec(memory_space=pltpu.VMEM)
    dma = pltpu.SemaphoreType.DMA
    hbm = pl.BlockSpec(memory_space=pltpu.HBM)
    sel_t, diag_t = pl.pallas_call(
        functools.partial(kernel, rows_n, cols_n),
        out_shape=(
            jax.ShapeDtypeStruct((snodes, wide, rows), F32),
            jax.ShapeDtypeStruct((snodes, wide, order), F32),
        ),
        in_specs=[hbm, vmem, vmem],
        out_specs=(vmem, vmem),
        scratch_shapes=[
            pltpu.VMEM(inverse_blocks.shape, BF16),
            pltpu.VMEM((2, cols_n * vb, rows), BF16),
            pltpu.VMEM((cols_n * vb, rows), BF16),
            pltpu.VMEM((y_n, 2 * vb, rows), F32),
            pltpu.VMEM((y_n, 2, vb, rows), I16),
            pltpu.VMEM((y_n, 2, 1, rows), F32),
            pltpu.VMEM((zh_n, X - 1, vb, rows), I16),
            pltpu.VMEM((zh_n, X - 1, 1, rows), F32),
            pltpu.VMEM((zh_n, vb, rows), F32),
            pltpu.VMEM((zh_n - 1, vb, rows), I16),
            pltpu.VMEM((zh_n - 1, 1, rows), F32),
            pltpu.VMEM((zh_n - 1, vb, rows), I16),
            pltpu.VMEM((zh_n - 1, 1, rows), F32),
            pltpu.VMEM((snodes, order, rows), BF16),
            pltpu.VMEM((tiles, 8, 128), F32),
            pltpu.VMEM((rows_n, 8, 128), F32),
            pltpu.VMEM((8, 128), F32),
            pltpu.VMEM((tiles, 8, 128), F32),
            dma,
            dma,
            dma,
            dma((y_n,)),
            dma((y_n,)),
            dma((y_n,)),
            dma((y_n,)),
            dma((2, y_n)),
            dma((2, y_n)),
            dma((zh_n - 1,)),
            dma((zh_n - 1,)),
            dma((zh_n, X - 1)),
            dma((zh_n, X - 1)),
            dma((2, y_n, 2)),
            dma((2, zh_n, X - 1)),
            dma((2, zh_n - 1)),
            dma((2, zh_n - 1)),
            dma((tiles,)),
            dma((rows_n,)),
            dma((rows_n,)),
            dma((tiles,)),
        ],
        compiler_params=pltpu.CompilerParams(
            collective_id=0, has_side_effects=True, vmem_limit_bytes=53 * 1024 * 1024
        ),
    )(inverse_blocks, panel_t, structure)
    return jnp.swapaxes(sel_t, 1, 2), diag_inverse - jnp.swapaxes(diag_t, 1, 2)


def solution(mesh):
    in_specs = (P("prow", "pcol"), P(None, "prow", "pcol"), P(None, None, "pcol"), P())
    out_specs = (P(None, "prow", "pcol"), P(None, None, "pcol"))
    step = functools.partial(body, mesh.shape["prow"], mesh.shape["pcol"])
    return jax.shard_map(step, mesh=mesh, in_specs=in_specs, out_specs=out_specs, check_vma=False)
```

time: 111 us -> 80.5 us (0.73)
  Pallas kernels: 105 us -> 76.8 us
  local copies, waits for them, and re-layouts: 5.4 us -> 2.22 us
    pallas_call x1, Pallas kernels: 105 us -> 76.8 us  [body(): pl.pallas_call(functools.partial(kernel, rows_n, cols_n), out_shape=(jax....]
    unnamed x10 -> x7, local copies, waits for them, and re-layouts: 5.4 us -> 2.22 us
where the time goes in v2:
time: 80.5 us; the launch traced here: 80.3 us
  Pallas kernels  76.8 us (95%)
  local copies, waits for them, and re-layouts  2.22 us (3%)
    pallas_call x1, Pallas kernels, body(): pl.pallas_call(functools.partial(kernel, rows_n, cols_n), out_shape=(jax....  76.8 us
    unnamed x7, local copies, waits for them, and re-layouts  2.22 us

profile of v2, /device:TPU:1, one launch (start us, length us, event | category | flops | bytes accessed | tf_op | source)
XLA Modules:
  0.0 80.3 jit_solution(16685836471952171638)
XLA Ops:
  0.6 0.0 copy-start
  0.6 0.9 %copy-done = bf16[2,768,24]{1,2,0:T(8,128)(2,1)S(1)} copy-done((bf16[2,768,24]{1,2,0:T(8,128)(2,1)S(1)}, bf16[2,768,24]{1,2,0:T(8,128)(2,1)}, u32[]{:S(2)}) %copy-start) | copy-done | bytes 73752
  1.5 0.0 copy-start.1
  1.5 0.7 copy-done.1
  2.2 0.0 copy-start.2
  2.2 76.8 %shard_map.59 = (f32[2,24,768]{2,1,0:T(8,128)S(1)}, f32[2,24,384]{2,1,0:T(8,128)S(1)}) custom-call(bf16[768,1536]{1,0:T(8,128)(2,1)} %a_hbm.1, bf16[2,24,768]{2,1,0:T(8,128)(2,1)S(1)} %bitcast.5, s32[2,48]{1,0:T(2,128)S(1)} %copy-done.1), custom_call_target="tpu_custom_call" | custom-call | tf_op jit(solution)/shard_map/pallas_call | solution.py:407
  79.0 0.0 copy-done.2
  79.0 0.6 bitcast_subtract_fusion
  79.6 0.7 copy.7
Async XLA Ops:
  0.6 0.9 %copy-start = (bf16[2,768,24]{1,2,0:T(8,128)(2,1)S(1)}, bf16[2,768,24]{1,2,0:T(8,128)(2,1)}, u32[]{:S(2)}) copy-start(bf16[2,768,24]{1,2,0:T(8,128)(2,1)} %param.5) | copy-start | bytes 221188
  1.5 0.7 copy-start.1
  2.2 76.8 %copy-start.2 = (f32[2,384,24]{1,2,0:T(8,128)S(1)}, f32[2,384,24]{1,2,0:T(8,128)}, u32[]{:S(2)}) copy-start(f32[2,384,24]{1,2,0:T(8,128)} %param.6) | copy-start | bytes 221188

commit v3 on v2

--- a/solution.py
+++ b/solution.py
@@ -54,8 +54,13 @@
     def row_of(yy, zz, cc):
         return lax.rem(yy + y_n, y_n) * 4 + zz * 2 + cc
 
-    partner = (row_of(p // 2 + q // 2, (p + q) % 2, core), p)
-    source = (q * 2 + core, mine)
+    shift = 2 * lax.rem(p // X - zh + zh_n + zh_n // 2, zh_n) + x // 2
+    partner = (row_of(p // 2 + shift, (p + x) % 2, core), p)
+
+    def z_of(index):
+        return lax.rem(zh + zh_n // 2 - index // 2 + zh_n, zh_n)
+
+    source = (q * 2 + core, z_of(depth) * X + 2 * (depth % 2) + parity)
     is_self = jnp.logical_and(partner[0] == prow, partner[1] == q)
     away = {o: (row_of(y + o, zl, core), q) for o in (1, -1, 2, -2)}
     across = (row_of(y, 1 - zl, core), q)
@@ -64,14 +69,14 @@
     zpeer = [(prow, lax.rem(zh + o, zh_n) * X + x) for o in range(1, zh_n)]
 
     barrier = pltpu.get_barrier_semaphore()
+    @pl.when(jnp.logical_not(is_self))
+    def _():
+        pl.semaphore_signal(barrier, inc=1, device_id=partner, device_id_type=MESH)
+        pl.semaphore_signal(barrier, inc=1, device_id=source, device_id_type=MESH)
+
     fixed = [*away.values(), across, sibling] + xpeer + zpeer
     for device in fixed:
         pl.semaphore_signal(barrier, inc=1, device_id=device, device_id_type=MESH)
-
-    @pl.when(jnp.logical_not(is_self))
-    def _():
-        pl.semaphore_signal(barrier, inc=1, device_id=partner, device_id_type=MESH)
-        pl.semaphore_signal(barrier, inc=1, device_id=source, device_id_type=MESH)
 
     load_a = pltpu.make_async_copy(a_hbm, a_ref, load_sem)
     load_a.start()
@@ -121,12 +126,12 @@
 
     @pl.when(is_self)
     def _():
-        pltpu.make_async_copy(own, slot(q), h_recv).start()
+        pltpu.make_async_copy(own, slot(2 * shift + x % 2), h_recv).start()
 
     @pl.when(jnp.logical_not(is_self))
     def _():
         pltpu.make_async_remote_copy(
-            src_ref=own, dst_ref=slot(q), send_sem=h_send, recv_sem=h_recv, device_id=partner, device_id_type=MESH
+            src_ref=own, dst_ref=slot(2 * shift + x % 2), send_sem=h_send, recv_sem=h_recv, device_id=partner, device_id_type=MESH
         ).start()
 
     def start_local():
@@ -187,17 +192,17 @@
 
             @pl.when(o == 0)
             def _():
-                acc[b // 2] = prod[n, i * vb : (i + 1) * vb, :]
+                acc[z_of(b)] = prod[n, i * vb : (i + 1) * vb, :]
 
             @pl.when(o > 0)
             def _():
                 code, scale = encode(prod[n, i * vb : (i + 1) * vb, :])
                 xs[n, i] = code
                 xs_scale[n, i] = scale
-                for k, (src, dst) in enumerate(((xs, xr), (xs_scale, xr_scale))):
+                for k, (src, dst) in ((1, (xs_scale, xr_scale)), (0, (xs, xr))):
                     pltpu.make_async_remote_copy(
-                        src_ref=src.at[n, i], dst_ref=dst.at[b // 2, o - 1], send_sem=x_send.at[k, n, i],
-                        recv_sem=x_recv.at[k, b // 2, o - 1], device_id=(prow, zh * X + to), device_id_type=MESH,
+                        src_ref=src.at[n, i], dst_ref=dst.at[z_of(b), o - 1], send_sem=x_send.at[k, n, i],
+                        recv_sem=x_recv.at[k, z_of(b), o - 1], device_id=(prow, zh * X + to), device_id_type=MESH,
                     ).start()
 
     high_x = x // 2
@@ -207,7 +212,7 @@
     def reduce_x(r):
         even_way, odd_way = ((0, -1), (-2, 1), (2, -3), (4, 3))[r - 1]
         b = lax.rem(depth + sign * ((1 - odd) * even_way + odd * odd_way) + y_n, y_n)
-        g = b // 2
+        g = z_of(b)
         total = acc[g]
         for o in range(X - 1):
             wait_for(xr.at[g, o], x_recv.at[0, g, o])
@@ -221,13 +226,15 @@
             code, scale = encode(acc[g])
             zs[o - 1] = code
             zs_scale[o - 1] = scale
-            for k, (src, dst) in enumerate(((zs, zr), (zs_scale, zr_scale))):
+            for k, (src, dst) in ((1, (zs_scale, zr_scale)), (0, (zs, zr))):
                 pltpu.make_async_remote_copy(
                     src_ref=src.at[o - 1], dst_ref=dst.at[o - 1], send_sem=z_send.at[k, o - 1],
                     recv_sem=z_recv.at[k, o - 1], device_id=(prow, g * X + x), device_id_type=MESH,
                 ).start()
 
     take_pair(0)
+    for o in range(1, zh_n):
+        pass_local(o)
     for offset in (-1, 1):
         take_y(offset)
         spread(offset)
@@ -240,8 +247,6 @@
     send(across_ring, across_ring, y_send.at[7], y_recv.at[7], (row_of(y + 2 * far, zl, core), q))
     for offset in (-2, 2):
         spread(offset)
-    for o in range(1, zh_n):
-        pass_local(o)
     load_a.wait()
     multiply(0)
     for offset in (-1, 1):

time: 80.5 us -> 77.6 us (0.964)
  Pallas kernels: 76.8 us -> 73.8 us
    pallas_call x1, Pallas kernels: 76.8 us -> 73.8 us  [body(): pl.pallas_call(functools.partial(kernel, rows_n, cols_n), out_shape=(jax....]
where the time goes in v3:
time: 77.6 us; the launch traced here: 77.4 us
  Pallas kernels  73.8 us (95%)
  local copies, waits for them, and re-layouts  2.22 us (3%)
    pallas_call x1, Pallas kernels, body(): pl.pallas_call(functools.partial(kernel, rows_n, cols_n), out_shape=(jax....  73.8 us
    unnamed x7, local copies, waits for them, and re-layouts  2.22 us

profile of v3, /device:TPU:1, one launch (start us, length us, event | category | flops | bytes accessed | tf_op | source)
XLA Modules:
  0.0 77.4 jit_solution(13307118516026860232)
XLA Ops:
  0.6 0.0 copy-start
  0.6 0.9 %copy-done = bf16[2,768,24]{1,2,0:T(8,128)(2,1)S(1)} copy-done((bf16[2,768,24]{1,2,0:T(8,128)(2,1)S(1)}, bf16[2,768,24]{1,2,0:T(8,128)(2,1)}, u32[]{:S(2)}) %copy-start) | copy-done | bytes 73752
  1.5 0.0 copy-start.1
  1.5 0.7 copy-done.1
  2.2 0.0 copy-start.2
  2.2 73.8 %shard_map.59 = (f32[2,24,768]{2,1,0:T(8,128)S(1)}, f32[2,24,384]{2,1,0:T(8,128)S(1)}) custom-call(bf16[768,1536]{1,0:T(8,128)(2,1)} %a_hbm.1, bf16[2,24,768]{2,1,0:T(8,128)(2,1)S(1)} %bitcast.5, s32[2,48]{1,0:T(2,128)S(1)} %copy-done.1), custom_call_target="tpu_custom_call" | custom-call | tf_op jit(solution)/shard_map/pallas_call | solution.py:412
  76.1 0.0 copy-done.2
  76.1 0.6 bitcast_subtract_fusion
  76.7 0.7 copy.7
Async XLA Ops:
  0.6 0.9 %copy-start = (bf16[2,768,24]{1,2,0:T(8,128)(2,1)S(1)}, bf16[2,768,24]{1,2,0:T(8,128)(2,1)}, u32[]{:S(2)}) copy-start(bf16[2,768,24]{1,2,0:T(8,128)(2,1)} %param.5) | copy-start | bytes 221188
  1.5 0.7 copy-start.1
  2.2 73.9 %copy-start.2 = (f32[2,384,24]{1,2,0:T(8,128)S(1)}, f32[2,384,24]{1,2,0:T(8,128)}, u32[]{:S(2)}) copy-start(f32[2,384,24]{1,2,0:T(8,128)} %param.6) | copy-start | bytes 221188

commit v4 on v3

--- a/solution.py
+++ b/solution.py
@@ -258,6 +258,7 @@
     for r in (2, 3):
         for offset in (-r, r):
             take_pair(offset)
+        for offset in (-r, r):
             multiply(offset)
     reduce_x(1)
     take_pair(4)

time: 77.6 us -> 79.2 us (1.021)
  Pallas kernels: 73.8 us -> 75.5 us
    pallas_call x1, Pallas kernels: 73.8 us -> 75.5 us  [body(): pl.pallas_call(functools.partial(kernel, rows_n, cols_n), out_shape=(jax....]
where the time goes in v4:
time: 79.2 us; the launch traced here: 79 us
  Pallas kernels  75.5 us (95%)
  local copies, waits for them, and re-layouts  2.22 us (3%)
    pallas_call x1, Pallas kernels, body(): pl.pallas_call(functools.partial(kernel, rows_n, cols_n), out_shape=(jax....  75.5 us
    unnamed x7, local copies, waits for them, and re-layouts  2.22 us

profile of v4, /device:TPU:1, one launch (start us, length us, event | category | flops | bytes accessed | tf_op | source)
XLA Modules:
  0.0 79.0 jit_solution(12979044855527205830)
XLA Ops:
  0.6 0.0 copy-start
  0.6 0.9 %copy-done = bf16[2,768,24]{1,2,0:T(8,128)(2,1)S(1)} copy-done((bf16[2,768,24]{1,2,0:T(8,128)(2,1)S(1)}, bf16[2,768,24]{1,2,0:T(8,128)(2,1)}, u32[]{:S(2)}) %copy-start) | copy-done | bytes 73752
  1.5 0.0 copy-start.1
  1.5 0.7 copy-done.1
  2.2 0.0 copy-start.2
  2.2 75.5 %shard_map.59 = (f32[2,24,768]{2,1,0:T(8,128)S(1)}, f32[2,24,384]{2,1,0:T(8,128)S(1)}) custom-call(bf16[768,1536]{1,0:T(8,128)(2,1)} %a_hbm.1, bf16[2,24,768]{2,1,0:T(8,128)(2,1)S(1)} %bitcast.5, s32[2,48]{1,0:T(2,128)S(1)} %copy-done.1), custom_call_target="tpu_custom_call" | custom-call | tf_op jit(solution)/shard_map/pallas_call | solution.py:413
  77.7 0.0 copy-done.2
  77.7 0.6 bitcast_subtract_fusion
  78.4 0.7 copy.7
Async XLA Ops:
  0.6 0.9 %copy-start = (bf16[2,768,24]{1,2,0:T(8,128)(2,1)S(1)}, bf16[2,768,24]{1,2,0:T(8,128)(2,1)}, u32[]{:S(2)}) copy-start(bf16[2,768,24]{1,2,0:T(8,128)(2,1)} %param.5) | copy-start | bytes 221188
  1.5 0.7 copy-start.1
  2.2 75.5 %copy-start.2 = (f32[2,384,24]{1,2,0:T(8,128)S(1)}, f32[2,384,24]{1,2,0:T(8,128)}, u32[]{:S(2)}) copy-start(f32[2,384,24]{1,2,0:T(8,128)} %param.6) | copy-start | bytes 221188
